TPU v7x, 32 devices: a whole 2x2x4 slice. The times are simulated.
32 devices in a mesh: groups: 2 (over x), ctx: 16 (over z, y, core).
Axes of the slice: x: 2, y: 2, z: 4, core: 2. Of those that a mesh axis runs over, the one named last changes fastest.
Arguments:
- queries: bfloat16 [4096, 768], P(('groups', 'ctx')), parts along dimension 0, may hold values from -80 to 80
- keys: bfloat16 [4096, 128], P(('groups', 'ctx')), parts along dimension 0, may hold values from -4 to 4
- values: bfloat16 [4096, 128], P(('groups', 'ctx')), parts along dimension 0, may hold values from -5 to 5
- out_grad: bfloat16 [4096, 768], P(('groups', 'ctx')), parts along dimension 0, may hold values from -5 to 5
- segment_ids: int32 [4096], P(('groups', 'ctx')), parts along dimension 0, may hold values from 0 to 5, never falling along the last dimension, each value on 1 to 512 neighbouring positions
- route: int32 [32, 16], P(('groups', 'ctx')), parts along dimension 0, may hold values from 0 to 15, each once within a row
Outputs:
- attended: bfloat16 [4096, 768], P(('groups', 'ctx')), parts along dimension 0
- query_grad: bfloat16 [4096, 768], P(('groups', 'ctx')), parts along dimension 0
- key_grad: bfloat16 [4096, 128], P(('groups', 'ctx')), parts along dimension 0
- value_grad: bfloat16 [4096, 128], P(('groups', 'ctx')), parts along dimension 0
There are 2 independent parts, one for each index of `groups`. A program takes and returns all parts, laid end to end along the dimension named above; each array names one. Nothing has to cross between parts.
Inputs may be any that keep to these rules, and one draw needn't show every extreme that they name: `segment_ids`: never falling along the pack; segment s belongs to DPO example s // 3 as its prompt (s % 3 == 0), chosen (1) or rejected (2) answer; each segment holds 1 to 512 tokens, one exactly that many. `route`: each row holds every number of its range once.
All inputs are finite; a program needn't handle non-finite values.
Results may differ from a plain program's by a relative error of at most 0.012.
The roundings to bfloat16 on the way count: a program that leaves them out, or rounds other values in their place, can miss the bound.
Values may be sent and summed in bfloat16 or wider, within the bound.
A program may use at most 64 MiB of HBM per device.

v0:
```python
import math

import jax
import jax.numpy as jnp
from jax import lax
from jax.sharding import PartitionSpec as P

big_negative = -1e30


def allowed_pairs(query_pos, query_seg, key_pos, key_seg):
    same_example = query_seg[:, None] // 3 == key_seg[None, :] // 3
    query_role = query_seg[:, None] % 3
    key_role = key_seg[None, :] % 3
    causal = key_pos[None, :] <= query_pos[:, None]
    return same_example & causal & ((key_role == query_role) | (key_role == 0))


def masked_scores(query_heads, key_block, allowed, factor):
    raw_score = (
        jnp.einsum("rhd,kd->hrk", query_heads, key_block, preferred_element_type=jnp.float32)
        * factor
    )
    return jnp.where(allowed[None], raw_score, big_negative)


def over_blocks(length, update, carried):
    blk_rows = math.gcd(length, 1024)
    turn_count = length // blk_rows
    return lax.fori_loop(
        0, turn_count, lambda turn, current: update(current, turn * blk_rows, blk_rows), carried
    )


def as_slots(row_array, send_rows, devices):
    return row_array[send_rows].reshape(
        (devices, send_rows.shape[0] // devices) + row_array.shape[1:]
    )


def from_slots(slots):
    return slots.reshape((slots.shape[0] * slots.shape[1],) + slots.shape[2:])


def body(queries, keys, values, out_grad, segment_ids, route):
    devices = lax.axis_size("ctx")
    row_count = queries.shape[0]
    head_dim = keys.shape[1]
    head_count = queries.shape[1] // head_dim
    factor = head_dim ** (-0.5)
    sub_rows = row_count // devices
    own_pos = lax.axis_index("ctx") * row_count + jnp.arange(row_count, dtype=jnp.int32)
    routing = route[0]
    send_rows = (
        routing[:, None] * sub_rows + jnp.arange(sub_rows, dtype=jnp.int32)[None, :]
    ).reshape(-1)
    arrived = (
        lax.all_to_all(
            as_slots(queries, send_rows, devices), "ctx", split_axis=0, concat_axis=0, tiled=True
        ),
        lax.all_to_all(
            as_slots(out_grad, send_rows, devices), "ctx", split_axis=0, concat_axis=0, tiled=True
        ),
        lax.all_to_all(
            as_slots(own_pos, send_rows, devices), "ctx", split_axis=0, concat_axis=0, tiled=True
        ),
        lax.all_to_all(
            as_slots(segment_ids, send_rows, devices),
            "ctx",
            split_axis=0,
            concat_axis=0,
            tiled=True,
        ),
    )
    query_rows = from_slots(arrived[0])
    grad_rows = from_slots(arrived[1])
    query_pos = from_slots(arrived[2])
    query_seg = from_slots(arrived[3])
    query_heads = query_rows.reshape(row_count, head_count, head_dim)
    grad_heads = grad_rows.reshape(row_count, head_count, head_dim)
    start_top = jnp.full((head_count, row_count), big_negative, jnp.float32)
    start_sum = jnp.zeros((head_count, row_count), jnp.float32)
    key_piece = lax.all_gather(keys, "ctx", axis=0, tiled=True)
    seg_piece = lax.all_gather(segment_ids, "ctx", axis=0, tiled=True)

    def stats_one_block(current, offset, blk_rows):
        key_block = lax.dynamic_slice_in_dim(key_piece, offset, blk_rows, 0)
        key_seg = lax.dynamic_slice_in_dim(seg_piece, offset, blk_rows, 0)
        key_pos = offset + jnp.arange(blk_rows, dtype=jnp.int32)
        allowed = allowed_pairs(query_pos, query_seg, key_pos, key_seg)

        def compute(running):
            row_top, denom_sum = running
            scores = masked_scores(query_heads, key_block, allowed, factor)
            new_top = jnp.maximum(row_top, jnp.max(scores, axis=2))
            denom_sum = denom_sum * jnp.exp(row_top - new_top) + jnp.sum(
                jnp.exp(scores - new_top[:, :, None]), axis=2
            )
            return (new_top, denom_sum)

        return lax.cond(jnp.any(allowed), compute, lambda running: running, current)

    row_top, denom_sum = over_blocks(key_piece.shape[0], stats_one_block, (start_top, start_sum))
    log_total = row_top + jnp.log(denom_sum)

    def fold_blocks(compute, carried, pieces):
        key_piece, value_piece, seg_piece = pieces

        def fold_one_block(current, offset, blk_rows):
            key_block = lax.dynamic_slice_in_dim(key_piece, offset, blk_rows, 0)
            value_block = lax.dynamic_slice_in_dim(value_piece, offset, blk_rows, 0)
            key_seg = lax.dynamic_slice_in_dim(seg_piece, offset, blk_rows, 0)
            key_pos = offset + jnp.arange(blk_rows, dtype=jnp.int32)
            allowed = allowed_pairs(query_pos, query_seg, key_pos, key_seg)
            return lax.cond(
                jnp.any(allowed),
                lambda running: compute(running, key_block, value_block, key_pos, allowed),
                lambda running: running,
                current,
            )

        return over_blocks(key_piece.shape[0], fold_one_block, carried)

    def visit_keys(compute, initial):
        return fold_blocks(
            compute,
            initial,
            (
                lax.all_gather(keys, "ctx", axis=0, tiled=True),
                lax.all_gather(values, "ctx", axis=0, tiled=True),
                lax.all_gather(segment_ids, "ctx", axis=0, tiled=True),
            ),
        )

    def output_work(running, key_block, value_block, key_pos, allowed):
        scores = masked_scores(query_heads, key_block, allowed, factor)
        prob_low = jnp.exp(scores - log_total[:, :, None]).astype(jnp.bfloat16)
        return running + jnp.einsum(
            "hrk,kd->rhd", prob_low, value_block, preferred_element_type=jnp.float32
        )

    zero_heads = jnp.zeros((row_count, head_count, head_dim), jnp.float32)
    attended_heads = visit_keys(output_work, zero_heads).astype(jnp.bfloat16)
    row_dots = jnp.sum(
        grad_heads.astype(jnp.float32) * attended_heads.astype(jnp.float32), axis=2
    ).T

    def grad_pieces(key_block, value_block, allowed):
        scores = masked_scores(query_heads, key_block, allowed, factor)
        attn_prob = jnp.exp(scores - log_total[:, :, None])
        grad_prob = jnp.einsum(
            "rhd,kd->hrk", grad_heads, value_block, preferred_element_type=jnp.float32
        )
        grad_score = (attn_prob * (grad_prob - row_dots[:, :, None])).astype(jnp.bfloat16)
        return (attn_prob, grad_score)

    def grad_work(running, key_block, value_block, key_pos, allowed):
        query_acc, key_terms = running
        attn_prob, grad_score = grad_pieces(key_block, value_block, allowed)
        prob_low = attn_prob.astype(jnp.bfloat16)
        query_acc = query_acc + jnp.einsum(
            "hrk,kd->rhd", grad_score, key_block, preferred_element_type=jnp.float32
        )
        key_part = (
            jnp.einsum("hrk,rhd->kd", grad_score, query_heads, preferred_element_type=jnp.float32)
            * factor
        )
        value_part = jnp.einsum(
            "hrk,rhd->kd", prob_low, grad_heads, preferred_element_type=jnp.float32
        )
        first_row = key_pos[0]
        former = lax.dynamic_slice_in_dim(key_terms, first_row, key_pos.shape[0], 0)
        key_terms = lax.dynamic_update_slice_in_dim(
            key_terms, former + jnp.concatenate([key_part, value_part], axis=1), first_row, 0
        )
        return (query_acc, key_terms)

    zero_terms = jnp.zeros((row_count * devices, 2 * head_dim), jnp.float32)
    query_acc, key_terms = visit_keys(grad_work, (zero_heads, zero_terms))
    reduced = lax.psum_scatter(key_terms, "ctx", scatter_dimension=0, tiled=True)
    key_grad = reduced[:, :head_dim].astype(jnp.bfloat16)
    value_grad = reduced[:, head_dim:].astype(jnp.bfloat16)
    attended_flat = attended_heads.reshape(row_count, head_count * head_dim)
    query_grad_flat = (
        (query_acc * factor).astype(jnp.bfloat16).reshape(row_count, head_count * head_dim)
    )
    attended, query_grad = (attended_flat, query_grad_flat)
    return (attended, query_grad, key_grad, value_grad)


def solution(mesh):
    in_specs = (
        P(("groups", "ctx"), None),
        P(("groups", "ctx"), None),
        P(("groups", "ctx"), None),
        P(("groups", "ctx"), None),
        P(("groups", "ctx")),
        P(("groups", "ctx"), None),
    )
    out_specs = (
        P(("groups", "ctx"), None),
        P(("groups", "ctx"), None),
        P(("groups", "ctx"), None),
        P(("groups", "ctx"), None),
    )
    return jax.shard_map(body, mesh=mesh, in_specs=in_specs, out_specs=out_specs, check_vma=False)
```

profile of v0, /device:TPU:0, one launch (start us, length us, event | category | flops | bytes accessed | tf_op | source)
XLA Modules:
  0.0 244.7 jit_solution(16060090916487026029)
XLA Ops:
  10.4 7.4 %all-to-all-start = ((s32[16,1,8]{2,1,0:T(1,128)}), s32[16,1,8]{2,1,0:T(1,128)S(1)}, u32[]{:S(2)}, u32[]{:S(2)}) async-start(s32[16,1,8]{2,1,0:T(1,128)} %bitcast.19), calls=%async_computation | async-start | bytes 16384 | tf_op jit(solution)/shard_map/all_to_all | solution.py:67
  19.8 4.4 %all-to-all-done = s32[16,1,8]{2,1,0:T(1,128)S(1)} async-done(((s32[16,1,8]{2,1,0:T(1,128)}), s32[16,1,8]{2,1,0:T(1,128)S(1)}, u32[]{:S(2)}, u32[]{:S(2)}) %all-to-all-start) | async-done | bytes 544 | tf_op jit(solution)/shard_map/all_to_all | solution.py:67
  24.2 3.5 %all-to-all-start.1 = ((s32[16,1,8]{2,1,0:T(1,128)}), s32[16,1,8]{2,1,0:T(1,128)S(1)}, u32[]{:S(2)}, u32[]{:S(2)}) async-start(s32[16,1,8]{2,1,0:T(1,128)} %bitcast.24), calls=%async_computation.1 | async-start | bytes 16384 | tf_op jit(solution)/shard_map/all_to_all | solution.py:64
  29.2 4.7 %all-to-all-done.1 = s32[16,1,8]{2,1,0:T(1,128)S(1)} async-done(((s32[16,1,8]{2,1,0:T(1,128)}), s32[16,1,8]{2,1,0:T(1,128)S(1)}, u32[]{:S(2)}, u32[]{:S(2)}) %all-to-all-start.1) | async-done | bytes 544 | tf_op jit(solution)/shard_map/all_to_all | solution.py:64
  33.9 3.5 %all-to-all-start.2 = ((bf16[16,8,768]{2,1,0:T(8,128)(2,1)}), bf16[16,8,768]{2,1,0:T(8,128)(2,1)S(1)}, u32[]{:S(2)}, u32[]{:S(2)}) async-start(bf16[16,8,768]{2,1,0:T(8,128)(2,1)} %bitcast.27), calls=%async_computation.2 | async-start | bytes 393216 | tf_op jit(solution)/shard_map/all_to_all | solution.py:58
  37.5 23.2 %all_gather.7 = bf16[2048,128]{1,0:T(8,128)(2,1)S(1)} all-gather(bf16[128,128]{1,0:T(8,128)(2,1)S(1)} %copy-done.6), channel_id=1, replica_groups=mesh['groups'=2,'ctx'=16] {'ctx'}, dimensions={0}, use_global_device_ids=true | all-gather | bytes 557056 | tf_op jit(solution)/shard_map/all_gather | solution.py:129
  62.3 17.3 %all-gather = s32[16,1,128]{2,1,0:T(1,128)S(1)} all-gather(s32[1,1,128]{2,1,0:T(1,128)S(1)} %bitcast.128), channel_id=1, replica_groups=mesh['groups'=2,'ctx'=16] {'ctx'}, dimensions={0}, use_global_device_ids=true | all-gather | bytes 8704 | tf_op jit(solution)/shard_map/all_gather | solution.py:131
  79.6 21.6 %all_gather.16 = bf16[2048,128]{1,0:T(8,128)(2,1)} all-gather(bf16[128,128]{1,0:T(8,128)(2,1)S(1)} %copy-done.7), channel_id=1, replica_groups=mesh['groups'=2,'ctx'=16] {'ctx'}, dimensions={0}, use_global_device_ids=true | all-gather | bytes 557056 | tf_op jit(solution)/shard_map/all_gather | solution.py:130
  102.6 3.5 %all-to-all-start.3 = ((bf16[16,8,768]{2,1,0:T(8,128)(2,1)}), bf16[16,8,768]{2,1,0:T(8,128)(2,1)S(1)}, u32[]{:S(2)}, u32[]{:S(2)}) async-start(bf16[16,8,768]{2,1,0:T(8,128)(2,1)} %bitcast.33), calls=%async_computation.3 | async-start | bytes 393216 | tf_op jit(solution)/shard_map/all_to_all | solution.py:61
  106.7 8.9 %while.58 = (s32[]{:T(128)}, f32[6,128]{1,0:T(8,128)S(1)}, f32[6,128]{1,0:T(8,128)S(1)}, s32[128,1]{0,1:T(1,128)}, s32[16,8]{1,0:T(8,128)S(1)}, /*index=5*/s32[2...) while((s32[]{:T(128)}, f32[6,128]{1,0:T(8,128)S(1)}, ...), condition=%wide.wide.region_6.7_spmd, body=%wide.wide.region_0.6_spmd.sunk | while | flops 207768448 | bytes 7226153 | solution.py:30
  116.2 10.9 %while.59 = (s32[]{:T(128)}, f32[128,6,128]{2,0,1:T(8,128)S(1)}, s32[128,1]{0,1:T(1,128)}, s32[16,8]{1,0:T(8,128)S(1)}, s32[2048]{0:T(1024)S(1)}, /*index=5*/s32...) while((s32[]{:T(128)}, f32[128,6,128]{2,0,1:T(8,128)S(1)}, ...), condition=%wide.wide.region_11.12_spmd, body=%wide.wide.region_7.11_spmd.sunk | while | flops 406832512 | bytes 1817365 | solution.py:30
  119.3 2.4 conditional.10
  119.3 2.3 fusion.12
  124.7 2.4 conditional.10
  124.8 2.3 fusion.12
  131.8 38.6 %while.60 = (s32[]{:T(128)}, f32[128,6,128]{2,0,1:T(8,128)S(1)}, f32[2048,256]{0,1:T(8,128)}, s32[128,1]{0,1:T(1,128)}, s32[16,8]{1,0:T(8,128)S(1)}, /*index=5*/...) while((s32[]{:T(128)}, f32[128,6,128]{2,0,1:T(8,128)S(1)}, ...), condition=%wide.wide.region_17.18_spmd, body=%wide.wide.region_13.17_spmd.sunk | while | flops 1016187264 | bytes 23266736 | solution.py:30
  132.6 2.2 fusion.82
  135.6 15.9 %conditional.11 = ((f32[128,6,128]{2,0,1:T(8,128)S(1)}, f32[2048,256]{0,1:T(8,128)})) conditional(s32[]{:T(128)} %convert_element_type.89, (f32[128,6,128]{2,0,1:T(8,128)S(1)}, f32[2048,256]{0,1:T(8,128)}) %tuple.254, (pred[128,1024]{0,1:T(8,128)(4,1)S(1)}, bf16[2048,128]{1,0:T(8,128)(2,1)S(1)}, s32[]{:T(128)}, ...), branch_computations={%region_15.15_spmd, %region_16.16_spmd} | conditional | flops 1015251968 | bytes 23088724 | solution.py:115
  145.7 5.8 %dynamic_update_slice.4 = f32[2048,256]{0,1:T(8,128)} dynamic-update-slice(f32[2048,256]{0,1:T(8,128)} %get-tuple-element.1042, f32[1024,256]{0,1:T(8,128)S(1)} %maximum_add_fusion, s32[]{:T(128)S(6)} %select_n.266, s32[]{:T(128)} %constant.332.clone) | dynamic-update-slice | bytes 2097156 | tf_op jit(solution)/shard_map/while/body/eval_jaxpr/cond/branch_1_fun/dynamic_update_slice | solution.py:173
  152.3 2.2 fusion.82
  155.2 15.2 %conditional.11 = ((f32[128,6,128]{2,0,1:T(8,128)S(1)}, f32[2048,256]{0,1:T(8,128)})) conditional(s32[]{:T(128)} %convert_element_type.89, (f32[128,6,128]{2,0,1:T(8,128)S(1)}, f32[2048,256]{0,1:T(8,128)}) %tuple.254, (pred[128,1024]{0,1:T(8,128)(4,1)S(1)}, bf16[2048,128]{1,0:T(8,128)(2,1)S(1)}, s32[]{:T(128)}, ...), branch_computations={%region_15.15_spmd, %region_16.16_spmd} | conditional | flops 1015251968 | bytes 23088724 | solution.py:115
  165.4 5.0 %dynamic_update_slice.4 = f32[2048,256]{0,1:T(8,128)} dynamic-update-slice(f32[2048,256]{0,1:T(8,128)} %get-tuple-element.1042, f32[1024,256]{0,1:T(8,128)S(1)} %maximum_add_fusion, s32[]{:T(128)S(6)} %select_n.266, s32[]{:T(128)} %constant.332.clone) | dynamic-update-slice | bytes 2097156 | tf_op jit(solution)/shard_map/while/body/eval_jaxpr/cond/branch_1_fun/dynamic_update_slice | solution.py:173
  170.4 2.9 %copy.76 = f32[2048,256]{1,0:T(8,128)} copy(f32[2048,256]{0,1:T(8,128)} %get-tuple-element.1074) | data formatting | bytes 4194304 | tf_op jit(solution)/shard_map/while | solution.py:30
  175.2 61.1 %reduce-scatter.2.cloned.1.call-done = f32[128,256]{1,0:T(8,128)} async-done(((f32[2048,256]{1,0:T(8,128)}), f32[128,256]{1,0:T(8,128)}) %reduce-scatter.2.cloned.1.call-update) | async-done | bytes 131088 | tf_op jit(solution)/shard_map/reduce_scatter | solution.py:180
  (126 shorter events, 51.5 us)
Async XLA Ops:
  7.2 20.5 %copy-start = (bf16[128,768]{1,0:T(8,128)(2,1)S(1)}, bf16[128,768]{1,0:T(8,128)(2,1)}, u32[]{:S(2)}) copy-start(bf16[128,768]{1,0:T(8,128)(2,1)} %param.18) | copy-start | bytes 589828
  7.2 55.1 %copy-start.1 = (s32[128]{0:T(128)S(1)}, s32[128]{0:T(128)}, u32[]{:S(2)}) copy-start(s32[128]{0:T(128)} %param.22) | copy-start | bytes 1540
  7.2 30.3 %copy-start.6 = (bf16[128,128]{1,0:T(8,128)(2,1)S(1)}, bf16[128,128]{1,0:T(8,128)(2,1)}, u32[]{:S(2)}) copy-start(bf16[128,128]{1,0:T(8,128)(2,1)} %param.19) | copy-start | bytes 98308
  7.2 53.5 %copy-start.2 = (bf16[128,768]{1,0:T(8,128)(2,1)S(1)}, bf16[128,768]{1,0:T(8,128)(2,1)}, u32[]{:S(2)}) copy-start(bf16[128,768]{1,0:T(8,128)(2,1)} %param.21) | copy-start | bytes 589828
  7.2 72.4 %copy-start.7 = (bf16[128,128]{1,0:T(8,128)(2,1)S(1)}, bf16[128,128]{1,0:T(8,128)(2,1)}, u32[]{:S(2)}) copy-start(bf16[128,128]{1,0:T(8,128)(2,1)} %param.20) | copy-start | bytes 98308
  10.4 13.7 %all-to-all-start = ((s32[16,1,8]{2,1,0:T(1,128)}), s32[16,1,8]{2,1,0:T(1,128)S(1)}, u32[]{:S(2)}, u32[]{:S(2)}) async-start(s32[16,1,8]{2,1,0:T(1,128)} %bitcast.19), calls=%async_computation | async-start | bytes 16384 | tf_op jit(solution)/shard_map/all_to_all | solution.py:67
  24.2 9.8 %all-to-all-start.1 = ((s32[16,1,8]{2,1,0:T(1,128)}), s32[16,1,8]{2,1,0:T(1,128)S(1)}, u32[]{:S(2)}, u32[]{:S(2)}) async-start(s32[16,1,8]{2,1,0:T(1,128)} %bitcast.24), calls=%async_computation.1 | async-start | bytes 16384 | tf_op jit(solution)/shard_map/all_to_all | solution.py:64
  33.9 72.7 %copy-start.5 = (s32[16,1,8]{2,1,0:T(1,128)}, s32[16,1,8]{2,1,0:T(1,128)S(1)}, u32[]{:S(2)}) copy-start(s32[16,1,8]{2,1,0:T(1,128)S(1)} %all-to-all-done.1) | copy-start | bytes 1540
  33.9 68.7 %all-to-all-start.2 = ((bf16[16,8,768]{2,1,0:T(8,128)(2,1)}), bf16[16,8,768]{2,1,0:T(8,128)(2,1)S(1)}, u32[]{:S(2)}, u32[]{:S(2)}) async-start(bf16[16,8,768]{2,1,0:T(8,128)(2,1)} %bitcast.27), calls=%async_computation.2 | async-start | bytes 393216 | tf_op jit(solution)/shard_map/all_to_all | solution.py:58
  102.6 24.9 %all-to-all-start.3 = ((bf16[16,8,768]{2,1,0:T(8,128)(2,1)}), bf16[16,8,768]{2,1,0:T(8,128)(2,1)S(1)}, u32[]{:S(2)}, u32[]{:S(2)}) async-start(bf16[16,8,768]{2,1,0:T(8,128)(2,1)} %bitcast.33), calls=%async_computation.3 | async-start | bytes 393216 | tf_op jit(solution)/shard_map/all_to_all | solution.py:61
  106.1 130.2 %reduce-scatter.2.cloned.1.call-start = ((), (), s32[]{:S(2)}) async-start(), calls=%async_computation.5 | async-start | bytes 2228224 | tf_op jit(solution)/shard_map/reduce_scatter | solution.py:180
  127.5 2.7 %copy-start.3 = (bf16[128,6,128]{0,2,1:T(8,128)(2,1)}, bf16[128,6,128]{0,2,1:T(8,128)(2,1)S(1)}, u32[]{:S(2)}) copy-start(bf16[128,6,128]{0,2,1:T(8,128)(2,1)S(1)} %copy.69) | copy-start | bytes 589828
  170.4 2.9 %copy-start.4 = (bf16[128,6,128]{0,2,1:T(8,128)(2,1)S(1)}, bf16[128,6,128]{0,2,1:T(8,128)(2,1)}, u32[]{:S(2)}) copy-start(bf16[128,6,128]{0,2,1:T(8,128)(2,1)} %copy-done.3) | copy-start | bytes 589828
Sparse Core Ops, SparseCore 0:
  173.5 62.8 reduce-scatter.1
where the time goes:
time: 246 us; the launch traced here: 245 us
  waiting for transfers between devices  70.3 us (29%)
  blocking collectives  62.1 us (25%)
  local copies, waits for them, and re-layouts  30.5 us (12%)
  other arithmetic  23.3 us (9%)
  starting transfers between devices  18.1 us (7%)
  matrix products  17.5 us (7%)
  between operations  14.3 us (6%)
  loops' own time  8.54 us (3%)
    reduce_scatter x1, waiting for transfers between devices, body(): lax.psum_scatter(key_terms, 'ctx', scatter_dimension=0, tiled=True)  61.1 us
    all_gather x1, blocking collectives, visit_keys(): lax.all_gather(keys, 'ctx', axis=0, tiled=True)  23.2 us
    all_gather x1, blocking collectives, visit_keys(): lax.all_gather(values, 'ctx', axis=0, tiled=True)  21.6 us
    all_gather x1, blocking collectives, visit_keys(): lax.all_gather(segment_ids, 'ctx', axis=0, tiled=True)  17.3 us
    dynamic_update_slice x2, local copies, waits for them, and re-layouts, grad_work(): lax.dynamic_update_slice_in_dim(key_terms, former + jnp.concatenate([key_...  10.8 us
    reduce_or x4, other arithmetic, fold_one_block(): jnp.any(allowed)  7.61 us
    all_to_all x1, starting transfers between devices, body(): lax.all_to_all(as_slots(segment_ids, send_rows, devices), 'ctx', split_ax...  7.39 us
    gather x4, local copies, waits for them, and re-layouts, as_slots(): row_array[send_rows]  5.9 us
  transfers between devices with their start and end apart: 5, of which 3 were waited for; matrix products, arithmetic and copies ran while one was open for 11% of the time, Pallas kernels for 0%

commit v1 on v0

v1 whole, which is shorter than its diff:
```python
import functools

import jax
import jax.numpy as jnp
from jax import lax
from jax.experimental import pallas as pl
from jax.experimental.pallas import tpu as pltpu
from jax.sharding import PartitionSpec as P

MESH = pl.DeviceIdType.MESH
F32 = jnp.float32
BF16 = jnp.bfloat16
big_negative = -1e30
reach = 3 * 512
pad_rows = 8
LANES = 256


def flip(block):
    return block.astype(F32).T.astype(BF16)


def product(left, right):
    return jnp.dot(left, right, preferred_element_type=F32)


def kernel(
    n, heads, factor, back, sub,
    q_ref, k_ref, v_ref, g_ref, seg_ref, route_ref,
    att_ref, dq_ref, kg_ref, vg_ref,
    kv, q_t, g_t, q_rows, g_rows, perm, score, prob, grad_score, top, total, out_t, dq_t,
    half_terms, own_terms, sib_out, sib_in, part_out, part_in, att_out, dq_out, att_in, dq_in,
    kv_send, kv_recv, fwd_send, fwd_recv, sib_send, sib_recv, part_send, part_recv,
    att_send, att_recv, dq_send, dq_recv,
):
    me = lax.axis_index("ctx")
    chip, core = lax.div(me, 2), lax.rem(me, 2)
    other = 1 - core
    sibling = chip * 2 + other
    chips = n // 2
    rows, dh = k_ref.shape
    columns = heads * rows
    far = jnp.minimum(chip, back)
    ahead = jnp.minimum(chips - 1 - chip, back)

    barrier = pltpu.get_barrier_semaphore()

    def greet(step, carry):
        pl.semaphore_signal(
            barrier, inc=1, device_id={"ctx": lax.rem(me + step, n)}, device_id_type=MESH
        )
        return carry

    lax.fori_loop(1, n, greet, 0)

    own_seg = seg_ref[...].astype(F32)
    kv[0, core, pl.ds(0, rows), :] = k_ref[...]
    kv[0, core, pl.ds(rows, rows), :] = v_ref[...]
    kv[0, core, pl.ds(2 * rows, 16), :] = jnp.broadcast_to(own_seg, (16, rows)).astype(BF16)
    pl.semaphore_wait(barrier, n - 1)

    def kv_copy(step, target):
        return pltpu.make_async_remote_copy(
            src_ref=kv.at[0, core], dst_ref=kv.at[step, core],
            send_sem=kv_send.at[step], recv_sem=kv_recv.at[step],
            device_id={"ctx": target}, device_id_type=MESH,
        )

    def fwd_copy(step, which):
        return pltpu.make_async_remote_copy(
            src_ref=kv.at[step, which], dst_ref=kv.at[step, which],
            send_sem=fwd_send.at[step], recv_sem=fwd_recv.at[step],
            device_id={"ctx": sibling}, device_id_type=MESH,
        )

    def sib_copy(step):
        return pltpu.make_async_remote_copy(
            src_ref=sib_out.at[step], dst_ref=sib_in.at[step],
            send_sem=sib_send.at[step], recv_sem=sib_recv.at[step],
            device_id={"ctx": sibling}, device_id_type=MESH,
        )

    def part_copy(step, target):
        return pltpu.make_async_remote_copy(
            src_ref=part_out.at[step], dst_ref=part_in.at[step],
            send_sem=part_send.at[step], recv_sem=part_recv.at[step],
            device_id={"ctx": target}, device_id_type=MESH,
        )

    def row_copy(outgoing, incoming, sends, recvs, step):
        target = lax.rem(me + step, n)
        return pltpu.make_async_remote_copy(
            src_ref=outgoing.at[target], dst_ref=incoming.at[me],
            send_sem=sends.at[step], recv_sem=recvs.at[step],
            device_id={"ctx": target}, device_id_type=MESH,
        )

    fwd_copy(0, core).start()

    def send_kv(step, carry):
        kv_copy(step, me + 2 * step).start()
        return carry

    lax.fori_loop(1, ahead + 1, send_kv, 0)

    for h in range(heads):
        part = slice(h * dh, (h + 1) * dh)
        block = slice(h * rows, (h + 1) * rows)
        q_h, g_h = q_ref[:, part], g_ref[:, part]
        q_t[:, block] = flip(q_h)
        g_t[:, block] = flip(g_h)
        q_rows[block, :] = q_h
        g_rows[block, :] = g_h

    slots = n * pad_rows
    spread = (
        lax.shift_right_logical(lax.broadcasted_iota(jnp.int32, (n, slots), 1), 3)
        == lax.broadcasted_iota(jnp.int32, (n, slots), 0)
    )
    routing = jnp.broadcast_to(route_ref[...].astype(F32), (16, n)).astype(BF16)
    block_of = product(routing, jnp.where(spread, 1.0, 0.0).astype(BF16))[:1]
    token = lax.broadcasted_iota(jnp.int32, (rows, slots), 1) & (pad_rows - 1)
    wanted = block_of * float(sub) + token.astype(F32)
    chosen = (wanted == lax.broadcasted_iota(jnp.int32, (rows, slots), 0).astype(F32)) & (token < sub)
    perm[...] = jnp.where(chosen, 1.0, 0.0).T.astype(BF16)

    top[...] = jnp.full_like(top, big_negative)
    prompt = jnp.floor((own_seg + 0.5) * (1.0 / 3.0)) * 3.0
    query_pos = lax.broadcasted_iota(jnp.int32, (rows, rows), 1) + core * rows
    key_row = lax.broadcasted_iota(jnp.int32, (rows, rows), 0)
    chunks = [slice(at, at + LANES) for at in range(0, columns, LANES)]

    def score_half(step, half):
        key_block = kv[step, half, pl.ds(0, rows), :]
        seg_tile = kv[step, half, pl.ds(2 * rows, 16), :].astype(F32)
        key_seg = jnp.broadcast_to(seg_tile[:1], (rows, rows)).T
        key_pos = key_row + (half * rows - step * 2 * rows)
        allowed = (key_pos <= query_pos) & ((key_seg == own_seg) | (key_seg == prompt))
        bias = jnp.where(allowed, 0.0, big_negative)
        bias = jnp.concatenate([bias] * (LANES // rows), axis=1)
        at = pl.ds(pl.multiple_of(half * rows, rows), rows)
        for chunk in chunks:
            values = product(key_block, q_t[:, chunk]) * factor + bias
            score[step, at, chunk] = values
            top[:, chunk] = jnp.maximum(
                top[:, chunk], jnp.max(values.reshape(rows // 8, 8, LANES), axis=0)
            )

    def scores(step, carry):
        @pl.when(step > 0)
        def _():
            kv_copy(step, me).wait_recv()
            fwd_copy(step, core).start()

        score_half(step, core)
        fwd_copy(step, other).wait_recv()
        score_half(step, other)
        return carry

    lax.fori_loop(0, far + 1, scores, 0)
    row_top = jnp.max(top[...], axis=0, keepdims=True)
    top[...] = jnp.broadcast_to(row_top, top.shape)
    total[...] = jnp.zeros_like(total)
    out_t[...] = jnp.zeros_like(out_t)
    dq_t[...] = jnp.zeros_like(dq_t)

    def sums(step, carry):
        for at in (pl.ds(0, rows), pl.ds(rows, rows)):
            for chunk in chunks:
                values = jnp.exp(score[step, at, chunk] - top[:1, chunk])
                score[step, at, chunk] = values
                total[:, chunk] += jnp.sum(values.reshape(rows // 8, 8, LANES), axis=0)
        return carry

    lax.fori_loop(0, far + 1, sums, 0)
    total[...] = jnp.broadcast_to(
        1.0 / jnp.sum(total[...], axis=0, keepdims=True), total.shape
    )

    def both(step, first):
        return jnp.concatenate(
            [kv[step, 0, pl.ds(first, rows), :], kv[step, 1, pl.ds(first, rows), :]], axis=0
        )

    def outputs(step, carry):
        value_t = flip(both(step, rows))
        for chunk in chunks:
            values = score[step, :, chunk] * total[:1, chunk]
            score[step, :, chunk] = values
            low = values.astype(BF16)
            prob[step, :, chunk] = low
            out_t[:, chunk] += product(value_t, low)
        return carry

    lax.fori_loop(0, far + 1, outputs, 0)

    def stage(transposed, outgoing, incoming, sends, recvs):
        pieces = []
        for h in range(heads):
            low = transposed[:, h * rows:(h + 1) * rows].astype(BF16)
            moved = lax.dot_general(
                perm[...], low, (((1,), (1,)), ((), ())), preferred_element_type=F32
            )
            pieces.append(moved.reshape(n, pad_rows, dh))
        for h in range(0, heads, 2):
            outgoing[:, h * pad_rows:(h + 2) * pad_rows, :] = jnp.concatenate(
                pieces[h:h + 2], axis=1
            ).astype(BF16)

        def send(step, carry):
            row_copy(outgoing, incoming, sends, recvs, step).start()
            return carry

        lax.fori_loop(1, n, send, 0)
        incoming[me] = outgoing[me]

    stage(out_t, att_out, att_in, att_send, att_recv)
    for chunk in chunks:
        low = out_t[:, chunk].astype(BF16).astype(F32)
        dots = jnp.sum(g_t[:, chunk].astype(F32) * low, axis=0, keepdims=True)
        top[:, chunk] = jnp.broadcast_to(dots, (8, LANES))

    def finish(step):
        sib_copy(step).wait_recv()
        own_terms[step] = own_terms[step] + sib_in[step].astype(F32)

        @pl.when(step > 0)
        def _():
            part_out[step] = own_terms[step].astype(BF16)
            part_copy(step, me - 2 * step).start()

    def grads(turn, carry):
        step = far - turn
        value_block, key_t = both(step, rows), flip(both(step, 0))
        for chunk in chunks:
            grad_prob = product(value_block, g_t[:, chunk])
            low = (score[step, :, chunk] * (grad_prob - top[:1, chunk])).astype(BF16)
            grad_score[:, chunk] = low
            dq_t[:, chunk] += product(key_t, low)
        key_part = product(grad_score[...], q_rows[...])
        value_part = product(prob[step], g_rows[...])
        for half in range(2):
            part = slice(half * rows, (half + 1) * rows)
            half_terms[half, :rows] = key_part[part]
            half_terms[half, rows:] = value_part[part]
        sib_out[step] = half_terms[other].astype(BF16)
        sib_copy(step).start()
        own_terms[step] = half_terms[core]

        @pl.when(turn > 0)
        def _():
            finish(step + 1)

        return carry

    lax.fori_loop(0, far + 1, grads, 0)
    dq_t[...] = dq_t[...] * factor
    stage(dq_t, dq_out, dq_in, dq_send, dq_recv)
    finish(0)

    def collect(incoming, outgoing, sends, recvs, result):
        def arrive(step, carry):
            row_copy(outgoing, incoming, sends, recvs, step).wait_recv()
            return carry

        lax.fori_loop(1, n, arrive, 0)
        if sub == pad_rows:
            for h in range(0, heads, 2):
                two = incoming[:, h * pad_rows:(h + 2) * pad_rows, :].astype(F32)
                for one in range(2):
                    result[:, (h + one) * dh:(h + one + 1) * dh] = (
                        two[:, one * pad_rows:(one + 1) * pad_rows]
                        .reshape(n * pad_rows, dh)
                        .astype(BF16)
                    )
        else:
            result[...] = incoming[...]

        def sent(step, carry):
            row_copy(outgoing, incoming, sends, recvs, step).wait_send()
            return carry

        lax.fori_loop(1, n, sent, 0)

    collect(att_in, att_out, att_send, att_recv, att_ref)

    def gather_part(step, carry):
        part_copy(step, me).wait_recv()
        own_terms[0] = own_terms[0] + part_in[step].astype(F32)
        return carry

    lax.fori_loop(1, ahead + 1, gather_part, 0)
    kg_ref[...] = (own_terms[0, :rows] * factor).astype(BF16)
    vg_ref[...] = own_terms[0, rows:].astype(BF16)
    collect(dq_in, dq_out, dq_send, dq_recv, dq_ref)

    def drain(step, carry):
        fwd_copy(step, core).wait_send()
        sib_copy(step).wait_send()
        return carry

    lax.fori_loop(0, far + 1, drain, 0)

    def drain_kv(step, carry):
        kv_copy(step, me).wait_send()
        return carry

    lax.fori_loop(1, ahead + 1, drain_kv, 0)

    def drain_parts(step, carry):
        part_copy(step, me).wait_send()
        return carry

    lax.fori_loop(1, far + 1, drain_parts, 0)


def body(n, queries, keys, values, out_grad, segment_ids, route):
    rows, dh = keys.shape
    heads = queries.shape[1] // dh
    sub = rows // n
    chips = n // 2
    back = min(-(-(reach - 1) // (2 * rows)), chips - 1)
    columns = heads * rows
    held = back + 1
    slots = n * pad_rows
    moved = (n, heads * pad_rows, dh)
    row_shape = queries.shape if sub == pad_rows else moved
    vmem = pl.BlockSpec(memory_space=pltpu.VMEM)
    dma = pltpu.SemaphoreType.DMA
    attended, query_grad, key_grad, value_grad = pl.pallas_call(
        functools.partial(kernel, n, heads, dh ** -0.5, back, sub),
        out_shape=(
            jax.ShapeDtypeStruct(row_shape, BF16),
            jax.ShapeDtypeStruct(row_shape, BF16),
            jax.ShapeDtypeStruct((rows, dh), BF16),
            jax.ShapeDtypeStruct((rows, dh), BF16),
        ),
        in_specs=[vmem] * 6,
        out_specs=(vmem,) * 4,
        scratch_shapes=[
            pltpu.VMEM((held, 2, 2 * rows + 16, dh), BF16),
            pltpu.VMEM((dh, columns), BF16),
            pltpu.VMEM((dh, columns), BF16),
            pltpu.VMEM((columns, dh), BF16),
            pltpu.VMEM((columns, dh), BF16),
            pltpu.VMEM((slots, rows), BF16),
            pltpu.VMEM((held, 2 * rows, columns), F32),
            pltpu.VMEM((held, 2 * rows, columns), BF16),
            pltpu.VMEM((2 * rows, columns), BF16),
            pltpu.VMEM((8, columns), F32),
            pltpu.VMEM((8, columns), F32),
            pltpu.VMEM((dh, columns), F32),
            pltpu.VMEM((dh, columns), F32),
            pltpu.VMEM((2, 2 * rows, dh), F32),
            pltpu.VMEM((held, 2 * rows, dh), F32),
            pltpu.VMEM((held, 2 * rows, dh), BF16),
            pltpu.VMEM((held, 2 * rows, dh), BF16),
            pltpu.VMEM((held, 2 * rows, dh), BF16),
            pltpu.VMEM((held, 2 * rows, dh), BF16),
            pltpu.VMEM(moved, BF16),
            pltpu.VMEM(moved, BF16),
            pltpu.VMEM(moved, BF16),
            pltpu.VMEM(moved, BF16),
        ]
        + [dma((held,))] * 8
        + [dma((n,))] * 4,
        compiler_params=pltpu.CompilerParams(
            collective_id=0, has_side_effects=True, vmem_limit_bytes=40 * 1024 * 1024
        ),
    )(queries, keys, values, out_grad, segment_ids.reshape(1, rows), route)
    if sub != pad_rows:

        def in_rows(block):
            split = block.reshape(n, heads, pad_rows, dh)[:, :, :sub]
            return split.transpose(0, 2, 1, 3).reshape(queries.shape)

        attended, query_grad = in_rows(attended), in_rows(query_grad)
    return attended, query_grad, key_grad, value_grad


def solution(mesh):
    rows = P(("groups", "ctx"), None)
    return jax.shard_map(
        functools.partial(body, mesh.shape["ctx"]),
        mesh=mesh,
        in_specs=(rows, rows, rows, rows, P(("groups", "ctx")), rows),
        out_specs=(rows, rows, rows, rows),
        check_vma=False,
    )
```

time: 246 us -> 53.4 us (0.22)
  waiting for transfers between devices: 70.3 us -> 0 us
  blocking collectives: 62.1 us -> 0 us
  Pallas kernels: 0 us -> 45.8 us
  local copies, waits for them, and re-layouts: 30.5 us -> 6.61 us
  other arithmetic: 23.3 us -> 0 us
  starting transfers between devices: 18.1 us -> 0 us
  matrix products: 17.5 us -> 0 us
  between operations: 14.3 us -> 0.66 us
  loops' own time: 8.54 us -> 0 us
    all_gather x3 -> x0, blocking collectives: 62.1 us -> none  [the longest x1 23.2 us: visit_keys(): lax.all_gather(keys, 'ctx', axis=0, tiled=True)]
    reduce_scatter x1 -> x0, waiting for transfers between devices: 61.1 us -> none  [body(): lax.psum_scatter(key_terms, 'ctx', scatter_dimension=0, tiled=True)]
    pallas_call x0 -> x1, Pallas kernels: none -> 45.8 us  [body(): pl.pallas_call(functools.partial(kernel, n, heads, dh ** (-0.5), back, su...]
    all_to_all x4 -> x0, starting transfers between devices: 17.9 us -> none  [the longest x1 7.39 us: body(): lax.all_to_all(as_slots(segment_ids, send_rows, devices), 'ctx', split_ax...]
    dot_general x14 -> x0, matrix products: 17.5 us -> none  [the longest x2 4.68 us: output_work(): jnp.einsum('hrk,kd->rhd', prob_low, value_block, preferred_element_type=j...]
    reduce_or x6 -> x0, other arithmetic: 10.8 us -> none  [the longest x4 7.61 us: fold_one_block(): jnp.any(allowed)]
    dynamic_update_slice x2 -> x0, local copies, waits for them, and re-layouts: 10.8 us -> none  [grad_work(): lax.dynamic_update_slice_in_dim(key_terms, former + jnp.concatenate([key_...]
    all_to_all x4 -> x0, waiting for transfers between devices: 9.14 us -> none  [the longest x1 4.74 us: body(): lax.all_to_all(as_slots(own_pos, send_rows, devices), 'ctx', split_axis=0...]
  transfers between devices with their start and end apart: 5 -> 0, of which waited for: 3 -> 0; matrix products, arithmetic and copies ran while one was open for 11% -> 0% of each run, Pallas kernels for 0% -> 0%
where the time goes in v1:
time: 53.4 us; the launch traced here: 53.1 us
  Pallas kernels  45.8 us (86%)
  local copies, waits for them, and re-layouts  6.61 us (12%)
  between operations  0.66 us (1%)
    pallas_call x1, Pallas kernels, body(): pl.pallas_call(functools.partial(kernel, n, heads, dh ** (-0.5), back, su...  45.8 us
    unnamed x16, local copies, waits for them, and re-layouts  6.61 us

profile of v1, /device:TPU:0, one launch (start us, length us, event | category | flops | bytes accessed | tf_op | source)
XLA Modules:
  0.0 53.1 jit_solution(15595305816451475571)
XLA Ops:
  0.6 0.0 copy-start.5
  0.6 0.0 copy-start.4
  0.7 0.6 %copy-done.5 = s32[1,16]{1,0:T(1,128)S(1)} copy-done((s32[1,16]{1,0:T(1,128)S(1)}, s32[1,16]{1,0:T(1,128)}, u32[]{:S(2)}) %copy-start.5) | copy-done | bytes 88
  1.3 0.0 copy-done.4
  1.3 0.0 copy-start
  1.3 0.9 %copy-done = bf16[128,768]{1,0:T(8,128)(2,1)S(1)} copy-done((bf16[128,768]{1,0:T(8,128)(2,1)S(1)}, bf16[128,768]{1,0:T(8,128)(2,1)}, u32[]{:S(2)}) %copy-start) | copy-done | bytes 196632
  2.2 0.0 copy-start.1
  2.2 0.9 %copy-done.1 = bf16[128,768]{1,0:T(8,128)(2,1)S(1)} copy-done((bf16[128,768]{1,0:T(8,128)(2,1)S(1)}, bf16[128,768]{1,0:T(8,128)(2,1)}, u32[]{:S(2)}) %copy-start.1) | copy-done | bytes 196632
  3.2 0.0 copy-start.2
  3.2 0.8 %copy-done.2 = bf16[128,128]{1,0:T(8,128)(2,1)S(1)} copy-done((bf16[128,128]{1,0:T(8,128)(2,1)S(1)}, bf16[128,128]{1,0:T(8,128)(2,1)}, u32[]{:S(2)}) %copy-start.2) | copy-done | bytes 32792
  3.9 0.0 copy-start.3
  3.9 0.8 %copy-done.3 = bf16[128,128]{1,0:T(8,128)(2,1)S(1)} copy-done((bf16[128,128]{1,0:T(8,128)(2,1)S(1)}, bf16[128,128]{1,0:T(8,128)(2,1)}, u32[]{:S(2)}) %copy-start.3) | copy-done | bytes 32792
  4.7 45.8 %shard_map.93 = (bf16[128,768]{1,0:T(8,128)(2,1)S(1)}, bf16[128,768]{1,0:T(8,128)(2,1)S(1)}, bf16[128,128]{1,0:T(8,128)(2,1)S(1)}, bf16[128,128]{1,0:T(8,128)(2,1)S(1)}) custom-call(bf16[128,768]{1,0:T(8,128)(2,1)S(1)} %copy-done, bf16[128,128]{1,0:T(8,128)(2,1)S(1)} %copy-done.2, bf16[128,128]{1,0:T(8,128)(2,1)S(1)} %copy-done.3, ...), custom_call_target="tpu_custom_call" | custom-call | tf_op jit(solution)/shard_map/pallas_call | solution.py:330
  50.5 0.7 %copy.14 = bf16[128,768]{1,0:T(8,128)(2,1)} copy(bf16[128,768]{1,0:T(8,128)(2,1)S(1)} %get-tuple-element.8) | data formatting | bytes 393216
  51.2 0.7 %copy.15 = bf16[128,768]{1,0:T(8,128)(2,1)} copy(bf16[128,768]{1,0:T(8,128)(2,1)S(1)} %get-tuple-element.9) | data formatting | bytes 393216
  51.8 0.6 %copy.16 = bf16[128,128]{1,0:T(8,128)(2,1)} copy(bf16[128,128]{1,0:T(8,128)(2,1)S(1)} %get-tuple-element.10) | data formatting | bytes 65536
  52.4 0.6 %copy.17 = bf16[128,128]{1,0:T(8,128)(2,1)} copy(bf16[128,128]{1,0:T(8,128)(2,1)S(1)} %get-tuple-element.11) | data formatting | bytes 65536
Async XLA Ops:
  0.6 0.7 %copy-start.5 = (s32[1,16]{1,0:T(1,128)S(1)}, s32[1,16]{1,0:T(1,128)}, u32[]{:S(2)}) copy-start(s32[1,16]{1,0:T(1,128)} %route_ref.1) | copy-start | bytes 196
  0.6 0.7 %copy-start.4 = (s32[128]{0:T(128)S(1)}, s32[128]{0:T(128)}, u32[]{:S(2)}) copy-start(s32[128]{0:T(128)} %param.10) | copy-start | bytes 1540
  1.3 0.9 %copy-start = (bf16[128,768]{1,0:T(8,128)(2,1)S(1)}, bf16[128,768]{1,0:T(8,128)(2,1)}, u32[]{:S(2)}) copy-start(bf16[128,768]{1,0:T(8,128)(2,1)} %q_ref.1) | copy-start | bytes 589828
  2.2 0.9 %copy-start.1 = (bf16[128,768]{1,0:T(8,128)(2,1)S(1)}, bf16[128,768]{1,0:T(8,128)(2,1)}, u32[]{:S(2)}) copy-start(bf16[128,768]{1,0:T(8,128)(2,1)} %g_ref.1) | copy-start | bytes 589828
  3.2 0.8 %copy-start.2 = (bf16[128,128]{1,0:T(8,128)(2,1)S(1)}, bf16[128,128]{1,0:T(8,128)(2,1)}, u32[]{:S(2)}) copy-start(bf16[128,128]{1,0:T(8,128)(2,1)} %k_ref.1) | copy-start | bytes 98308
  3.9 0.8 %copy-start.3 = (bf16[128,128]{1,0:T(8,128)(2,1)S(1)}, bf16[128,128]{1,0:T(8,128)(2,1)}, u32[]{:S(2)}) copy-start(bf16[128,128]{1,0:T(8,128)(2,1)} %v_ref.1) | copy-start | bytes 98308

commit v2 on v1

--- a/solution.py
+++ b/solution.py
@@ -26,8 +26,9 @@
 
 def kernel(
     n, heads, factor, back, sub,
-    q_ref, k_ref, v_ref, g_ref, seg_ref, route_ref,
+    q_hbm, k_hbm, v_hbm, g_hbm, seg_hbm, route_hbm,
     att_ref, dq_ref, kg_ref, vg_ref,
+    q_ref, g_ref, seg_ref, route_ref, load_sem,
     kv, q_t, g_t, q_rows, g_rows, perm, score, prob, grad_score, top, total, out_t, dq_t,
     half_terms, own_terms, sib_out, sib_in, part_out, part_in, att_out, dq_out, att_in, dq_in,
     kv_send, kv_recv, fwd_send, fwd_recv, sib_send, sib_recv, part_send, part_recv,
@@ -38,11 +39,24 @@
     other = 1 - core
     sibling = chip * 2 + other
     chips = n // 2
-    rows, dh = k_ref.shape
+    rows, dh = k_hbm.shape
     columns = heads * rows
     far = jnp.minimum(chip, back)
     ahead = jnp.minimum(chips - 1 - chip, back)
 
+    loads = [
+        pltpu.make_async_copy(source, held, load_sem.at[at])
+        for at, (source, held) in enumerate((
+            (k_hbm, kv.at[0, core, pl.ds(0, rows)]),
+            (v_hbm, kv.at[0, core, pl.ds(rows, rows)]),
+            (seg_hbm, seg_ref),
+            (route_hbm, route_ref),
+            (q_hbm, q_ref),
+            (g_hbm, g_ref),
+        ))
+    ]
+    for load in loads:
+        load.start()
     barrier = pltpu.get_barrier_semaphore()
 
     def greet(step, carry):
@@ -53,15 +67,15 @@
 
     lax.fori_loop(1, n, greet, 0)
 
+    for load in loads[:3]:
+        load.wait()
     own_seg = seg_ref[...].astype(F32)
-    kv[0, core, pl.ds(0, rows), :] = k_ref[...]
-    kv[0, core, pl.ds(rows, rows), :] = v_ref[...]
     kv[0, core, pl.ds(2 * rows, 16), :] = jnp.broadcast_to(own_seg, (16, rows)).astype(BF16)
     pl.semaphore_wait(barrier, n - 1)
 
-    def kv_copy(step, target):
+    def kv_copy(source, step, target):
         return pltpu.make_async_remote_copy(
-            src_ref=kv.at[0, core], dst_ref=kv.at[step, core],
+            src_ref=kv.at[source, core], dst_ref=kv.at[step, core],
             send_sem=kv_send.at[step], recv_sem=kv_recv.at[step],
             device_id={"ctx": target}, device_id_type=MESH,
         )
@@ -97,12 +111,35 @@
 
     fwd_copy(0, core).start()
 
+    odd = lax.rem(chip, 2)
+    partner = me + 2 - 4 * odd
+    ahead_even = lax.div(ahead, 2)
+
     def send_kv(step, carry):
-        kv_copy(step, me + 2 * step).start()
-        return carry
-
-    lax.fori_loop(1, ahead + 1, send_kv, 0)
-
+        kv_copy(0, 2 * step, me + 4 * step).start()
+        return carry
+
+    lax.fori_loop(1, ahead_even + 1, send_kv, 0)
+
+    def for_partner(step):
+        there = step + 1 - 2 * odd
+        return there, (lax.rem(step, 2) == 0) & (there >= 0) & (there <= back)
+
+    def relay(step, finished):
+        there, needed = for_partner(step)
+
+        @pl.when(needed)
+        def _():
+            copy = kv_copy(step, there, partner)
+            if finished:
+                copy.wait_send()
+            else:
+                copy.start()
+
+    relay(0, False)
+
+    for load in loads[3:]:
+        load.wait()
     for h in range(heads):
         part = slice(h * dh, (h + 1) * dh)
         block = slice(h * rows, (h + 1) * rows)
@@ -146,10 +183,15 @@
                 top[:, chunk], jnp.max(values.reshape(rows // 8, 8, LANES), axis=0)
             )
 
-    def scores(step, carry):
+    evens = lax.div(far, 2) + 1
+
+    def scores(turn, carry):
+        step = jnp.where(turn < evens, 2 * turn, 2 * (turn - evens) + 1)
+
         @pl.when(step > 0)
         def _():
-            kv_copy(step, me).wait_recv()
+            kv_copy(0, step, me).wait_recv()
+            relay(step, False)
             fwd_copy(step, core).start()
 
         score_half(step, core)
@@ -295,6 +337,7 @@
     collect(dq_in, dq_out, dq_send, dq_recv, dq_ref)
 
     def drain(step, carry):
+        relay(step, True)
         fwd_copy(step, core).wait_send()
         sib_copy(step).wait_send()
         return carry
@@ -302,10 +345,10 @@
     lax.fori_loop(0, far + 1, drain, 0)
 
     def drain_kv(step, carry):
-        kv_copy(step, me).wait_send()
-        return carry
-
-    lax.fori_loop(1, ahead + 1, drain_kv, 0)
+        kv_copy(0, 2 * step, me).wait_send()
+        return carry
+
+    lax.fori_loop(1, ahead_even + 1, drain_kv, 0)
 
     def drain_parts(step, carry):
         part_copy(step, me).wait_send()
@@ -319,7 +362,8 @@
     heads = queries.shape[1] // dh
     sub = rows // n
     chips = n // 2
-    back = min(-(-(reach - 1) // (2 * rows)), chips - 1)
+    back = -(-(reach - 1) // (2 * rows))
+    back = min(back + back % 2, chips - 1)
     columns = heads * rows
     held = back + 1
     slots = n * pad_rows
@@ -335,9 +379,14 @@
             jax.ShapeDtypeStruct((rows, dh), BF16),
             jax.ShapeDtypeStruct((rows, dh), BF16),
         ),
-        in_specs=[vmem] * 6,
+        in_specs=[pl.BlockSpec(memory_space=pltpu.HBM)] * 6,
         out_specs=(vmem,) * 4,
         scratch_shapes=[
+            pltpu.VMEM(queries.shape, BF16),
+            pltpu.VMEM(queries.shape, BF16),
+            pltpu.VMEM((1, rows), jnp.int32),
+            pltpu.VMEM(route.shape, jnp.int32),
+            dma((6,)),
             pltpu.VMEM((held, 2, 2 * rows + 16, dh), BF16),
             pltpu.VMEM((dh, columns), BF16),
             pltpu.VMEM((dh, columns), BF16),

time: 53.4 us -> 49.1 us (0.919)
  Pallas kernels: 45.8 us -> 41.5 us
    pallas_call x1, Pallas kernels: 45.8 us -> 41.5 us  [body(): pl.pallas_call(functools.partial(kernel, n, heads, dh ** (-0.5), back, su...]
where the time goes in v2:
time: 49.1 us; the launch traced here: 48.7 us
  Pallas kernels  41.5 us (85%)
  local copies, waits for them, and re-layouts  6.61 us (13%)
  between operations  0.66 us (1%)
    pallas_call x1, Pallas kernels, body(): pl.pallas_call(functools.partial(kernel, n, heads, dh ** (-0.5), back, su...  41.5 us
    unnamed x16, local copies, waits for them, and re-layouts  6.61 us

profile of v2, /device:TPU:0, one launch (start us, length us, event | category | flops | bytes accessed | tf_op | source)
XLA Modules:
  0.0 48.7 jit_solution(14218937693293116831)
XLA Ops:
  0.6 0.0 copy-start.5
  0.6 0.0 copy-start.4
  0.7 0.6 %copy-done.5 = s32[1,16]{1,0:T(1,128)S(1)} copy-done((s32[1,16]{1,0:T(1,128)S(1)}, s32[1,16]{1,0:T(1,128)}, u32[]{:S(2)}) %copy-start.5) | copy-done | bytes 88
  1.3 0.0 copy-done.4
  1.3 0.0 copy-start
  1.3 0.9 %copy-done = bf16[128,768]{1,0:T(8,128)(2,1)S(1)} copy-done((bf16[128,768]{1,0:T(8,128)(2,1)S(1)}, bf16[128,768]{1,0:T(8,128)(2,1)}, u32[]{:S(2)}) %copy-start) | copy-done | bytes 196632
  2.2 0.0 copy-start.1
  2.2 0.9 %copy-done.1 = bf16[128,768]{1,0:T(8,128)(2,1)S(1)} copy-done((bf16[128,768]{1,0:T(8,128)(2,1)S(1)}, bf16[128,768]{1,0:T(8,128)(2,1)}, u32[]{:S(2)}) %copy-start.1) | copy-done | bytes 196632
  3.2 0.0 copy-start.2
  3.2 0.8 %copy-done.2 = bf16[128,128]{1,0:T(8,128)(2,1)S(1)} copy-done((bf16[128,128]{1,0:T(8,128)(2,1)S(1)}, bf16[128,128]{1,0:T(8,128)(2,1)}, u32[]{:S(2)}) %copy-start.2) | copy-done | bytes 32792
  3.9 0.0 copy-start.3
  3.9 0.8 %copy-done.3 = bf16[128,128]{1,0:T(8,128)(2,1)S(1)} copy-done((bf16[128,128]{1,0:T(8,128)(2,1)S(1)}, bf16[128,128]{1,0:T(8,128)(2,1)}, u32[]{:S(2)}) %copy-start.3) | copy-done | bytes 32792
  4.7 41.5 %shard_map.93 = (bf16[128,768]{1,0:T(8,128)(2,1)S(1)}, bf16[128,768]{1,0:T(8,128)(2,1)S(1)}, bf16[128,128]{1,0:T(8,128)(2,1)S(1)}, bf16[128,128]{1,0:T(8,128)(2,1)S(1)}) custom-call(bf16[128,768]{1,0:T(8,128)(2,1)S(1)} %copy-done, bf16[128,128]{1,0:T(8,128)(2,1)S(1)} %copy-done.2, bf16[128,128]{1,0:T(8,128)(2,1)S(1)} %copy-done.3, ...), custom_call_target="tpu_custom_call" | custom-call | tf_op jit(solution)/shard_map/pallas_call | solution.py:374
  46.2 0.7 %copy.14 = bf16[128,768]{1,0:T(8,128)(2,1)} copy(bf16[128,768]{1,0:T(8,128)(2,1)S(1)} %get-tuple-element.8) | data formatting | bytes 393216
  46.8 0.7 %copy.15 = bf16[128,768]{1,0:T(8,128)(2,1)} copy(bf16[128,768]{1,0:T(8,128)(2,1)S(1)} %get-tuple-element.9) | data formatting | bytes 393216
  47.5 0.6 %copy.16 = bf16[128,128]{1,0:T(8,128)(2,1)} copy(bf16[128,128]{1,0:T(8,128)(2,1)S(1)} %get-tuple-element.10) | data formatting | bytes 65536
  48.1 0.6 %copy.17 = bf16[128,128]{1,0:T(8,128)(2,1)} copy(bf16[128,128]{1,0:T(8,128)(2,1)S(1)} %get-tuple-element.11) | data formatting | bytes 65536
Async XLA Ops:
  0.6 0.7 %copy-start.5 = (s32[1,16]{1,0:T(1,128)S(1)}, s32[1,16]{1,0:T(1,128)}, u32[]{:S(2)}) copy-start(s32[1,16]{1,0:T(1,128)} %route_hbm.1) | copy-start | bytes 196
  0.6 0.7 %copy-start.4 = (s32[128]{0:T(128)S(1)}, s32[128]{0:T(128)}, u32[]{:S(2)}) copy-start(s32[128]{0:T(128)} %param.10) | copy-start | bytes 1540
  1.3 0.9 %copy-start = (bf16[128,768]{1,0:T(8,128)(2,1)S(1)}, bf16[128,768]{1,0:T(8,128)(2,1)}, u32[]{:S(2)}) copy-start(bf16[128,768]{1,0:T(8,128)(2,1)} %q_hbm.1) | copy-start | bytes 589828
  2.2 0.9 %copy-start.1 = (bf16[128,768]{1,0:T(8,128)(2,1)S(1)}, bf16[128,768]{1,0:T(8,128)(2,1)}, u32[]{:S(2)}) copy-start(bf16[128,768]{1,0:T(8,128)(2,1)} %g_hbm.1) | copy-start | bytes 589828
  3.2 0.8 %copy-start.2 = (bf16[128,128]{1,0:T(8,128)(2,1)S(1)}, bf16[128,128]{1,0:T(8,128)(2,1)}, u32[]{:S(2)}) copy-start(bf16[128,128]{1,0:T(8,128)(2,1)} %k_hbm.1) | copy-start | bytes 98308
  3.9 0.8 %copy-start.3 = (bf16[128,128]{1,0:T(8,128)(2,1)S(1)}, bf16[128,128]{1,0:T(8,128)(2,1)}, u32[]{:S(2)}) copy-start(bf16[128,128]{1,0:T(8,128)(2,1)} %v_hbm.1) | copy-start | bytes 98308
